TPU v7x, 512 devices: a whole 4x8x8 slice. The times are simulated.
512 devices in a mesh: ctx: 32 (over x, z), hg: 16 (over y, core).
Axes of the slice: x: 4, y: 8, z: 8, core: 2. Of those that a mesh axis runs over, the one named last changes fastest.
Arguments:
- query_nope: bfloat16 [128, 128, 128], P('ctx', 'hg'), may hold values from -6 to 6
- query_rope: bfloat16 [128, 128, 64], P('ctx', 'hg'), may hold values from -160 to 160
- latent: bfloat16 [24576, 512], P('ctx'), may hold values from -6 to 6
- key_rope: bfloat16 [24576, 64], P('ctx'), may hold values from -160 to 160
- up_keys: bfloat16 [512, 128, 128], P(None, 'hg'), may hold values from -0.25 to 0.25
- up_values: bfloat16 [512, 128, 128], P(None, 'hg'), may hold values from -0.25 to 0.25
- out_weight: bfloat16 [128, 128, 7168], P('hg', None, 'ctx'), may hold values from -0.046875 to 0.046875
- live_rows: int32 [32], P('ctx'), may hold values from 1 to 768, 18432 in all
- span_start: int32 [1], replicated, may hold values from 9216 to 18304
Outputs:
- mixed: bfloat16 [128, 7168], P('hg', 'ctx')
Inputs may be any that keep to these rules, and one draw needn't show every extreme that they name: `live_rows`: the values sum to 18432.
All inputs are finite; a program needn't handle non-finite values. No bound on the sum of `live_rows` on one device may be relied on, other than what follows from the above.
Results may differ from a plain program's by a relative error of at most 0.0082.
Values may be sent and summed in bfloat16 or wider, within the bound.
A program may use at most 64 MiB of HBM per device.

v0:
```python
import math

import jax
import jax.numpy as jnp
from jax import lax
from jax.sharding import PartitionSpec as P

NEG = -1e30


def prefix(x, axis, combine, identity):
    size, mine = (lax.axis_size(axis), lax.axis_index(axis))
    everything = lax.all_gather(x, axis)
    start = jnp.broadcast_to(jnp.asarray(identity, x.dtype), x.shape)

    def step(k, before):
        reached = k < mine
        new = combine(before, everything[k])
        return jnp.where(reached, new, before)

    return lax.fori_loop(0, size, step, start)


def add_counts(earlier, later):
    return earlier + later


def attend_local(
    query_nope, query_rope, latent, key_rope, up_keys, up_values, positions, offset, count
):
    factor = 1.0 / math.sqrt(query_nope.shape[-1] + query_rope.shape[-1])
    index = jnp.arange(latent.shape[0], dtype=jnp.int32)
    visible = (index < count)[None, :] & ((offset + index)[None, :] <= positions[:, None])
    nope_heads = jnp.transpose(query_nope, (1, 0, 2))
    rope_heads = jnp.transpose(query_rope, (1, 0, 2))
    key_maps = jnp.transpose(up_keys, (1, 0, 2))
    value_maps = jnp.transpose(up_values, (1, 0, 2))

    def one_head(inputs):
        nope_one, rope_one, key_map, value_map = inputs
        keys_one = jnp.dot(latent, key_map, preferred_element_type=jnp.float32).astype(jnp.bfloat16)
        values_one = jnp.dot(latent, value_map, preferred_element_type=jnp.float32).astype(
            jnp.bfloat16
        )
        scores = jnp.dot(nope_one, keys_one.T, preferred_element_type=jnp.float32)
        scores = (
            scores + jnp.dot(rope_one, key_rope.T, preferred_element_type=jnp.float32)
        ) * factor
        scores = jnp.where(visible, scores, NEG)
        maxima = jnp.max(scores, axis=1)
        weights = jnp.where(visible, jnp.exp(scores - maxima[:, None]), 0.0)
        totals = jnp.sum(weights, axis=1)
        output = jnp.dot(
            weights.astype(jnp.bfloat16), values_one, preferred_element_type=jnp.float32
        )
        return (maxima, totals, output)

    maxima, totals, output = lax.map(one_head, (nope_heads, rope_heads, key_maps, value_maps))
    return (maxima.T, totals.T, jnp.transpose(output, (1, 0, 2)))


def per_device(
    query_nope, query_rope, latent, key_rope, up_keys, up_values, out_weight, live_rows, span_start
):
    nope_all, rope_all = (
        lax.all_gather(query_nope, "ctx", axis=0, tiled=True),
        lax.all_gather(query_rope, "ctx", axis=0, tiled=True),
    )
    offset = prefix(live_rows, "ctx", add_counts, jnp.zeros_like(live_rows))
    count = live_rows[0]
    first_pos = offset[0]
    tokens = nope_all.shape[0]
    heads = nope_all.shape[1]
    vwidth = up_values.shape[2]
    positions = span_start[0] + jnp.arange(tokens, dtype=jnp.int32)
    maxima, totals, output = attend_local(
        nope_all, rope_all, latent, key_rope, up_keys, up_values, positions, first_pos, count
    )
    overall = lax.pmax(maxima, "ctx")
    rescale = jnp.exp(maxima - overall)
    totals, output = lax.psum((totals * rescale, output * rescale[:, :, None]), "ctx")
    attn = (output / totals[:, :, None]).astype(jnp.bfloat16).reshape(tokens, heads * vwidth)
    flat_weight = out_weight.reshape(heads * vwidth, out_weight.shape[2])
    mixed = lax.psum_scatter(
        jnp.dot(attn, flat_weight, preferred_element_type=jnp.float32),
        "hg",
        scatter_dimension=0,
        tiled=True,
    )
    return mixed.astype(jnp.bfloat16)


def solution(mesh):
    placed = (
        P("ctx", "hg", None),
        P("ctx", "hg", None),
        P("ctx", None),
        P("ctx", None),
        P(None, "hg", None),
        P(None, "hg", None),
        P("hg", None, "ctx"),
        P("ctx"),
        P(),
    )
    return jax.shard_map(
        per_device, mesh=mesh, in_specs=placed, out_specs=P("hg", "ctx"), check_vma=False
    )
```

profile of v0, /device:TPU:1, one launch (start us, length us, event | category | flops | bytes accessed | tf_op | source)
XLA Modules:
  0.0 501.5 jit_solution(15922641224006966708)
XLA Ops:
  7.3 1.3 dynamic-slice
  9.2 22.7 %all-reduce = s32[32]{0:T(128)S(1)} all-reduce(s32[32]{0:T(128)S(1)} %dynamic-update-slice), channel_id=2, replica_groups=mesh['ctx'=32,'hg'=16] {'ctx'}, use_global_device_ids=true, to_apply=%add | all-reduce | flops 32 | bytes 256
  31.9 41.8 %while.28 = (s32[]{:T(128)}, s32[1]{0:T(128)}, s32[]{:T(128)}, s32[32,1]{0,1:T(1,128)S(1)}, s32[]{:T(128)}) while((s32[]{:T(128)}, s32[1]{0:T(128)}, s32[]{:T(128)}, s32[32,1]{0,1:T(1,128)S(1)}, s32[]{:T(128)}) %tuple.62), condition=%wide.region_1.2_spmd, body=%wide.region_0.1_spmd.sunk | while | flops 5 | bytes 107 | solution.py:21
  73.7 35.4 %all_gather.12 = bf16[128,8,128]{2,1,0:T(8,128)(2,1)S(1)} all-gather(bf16[4,8,128]{2,1,0:T(8,128)(2,1)S(1)} %copy-done.4), channel_id=1, replica_groups=mesh['ctx'=32,'hg'=16] {'ctx'}, dimensions={0}, use_global_device_ids=true | all-gather | bytes 270336 | tf_op jit(solution)/shard_map/all_gather | solution.py:66
  109.2 35.5 %all_gather.13 = bf16[128,8,64]{2,1,0:T(8,128)(2,1)S(1)} all-gather(bf16[4,8,64]{2,1,0:T(8,128)(2,1)S(1)} %copy-done.5), channel_id=1, replica_groups=mesh['ctx'=32,'hg'=16] {'ctx'}, dimensions={0}, use_global_device_ids=true | all-gather | bytes 135168 | tf_op jit(solution)/shard_map/all_gather | solution.py:67
  146.2 2.6 copy_bitcast_fusion
  148.7 32.7 %while.29 = (s32[]{:T(128)}, f32[8,128]{1,0:T(8,128)S(1)}, f32[8,128]{1,0:T(8,128)S(1)}, f32[8,128,128]{2,1,0:T(8,128)}, bf16[8,128,128]{2,1,0:T(8,128)(2,1)S(1)...) while((s32[]{:T(128)}, f32[8,128]{1,0:T(8,128)S(1)}, ...), condition=%wide.region_5.6_spmd.clone, body=%wide.region_2.5_spmd.clone.sunk | while | flops 266010368 | bytes 4050325 | solution.py:58
  150.4 2.1 fusion.61
  154.5 2.1 fusion.61
  158.5 2.1 fusion.61
  162.6 2.1 fusion.61
  165.7 1.1 fusion.59
  166.7 2.1 fusion.61
  170.8 2.1 fusion.61
  173.8 1.1 fusion.59
  174.9 2.1 fusion.61
  179.0 2.1 fusion.61
  181.4 58.5 %pmax.7 = f32[128,8]{0,1:T(8,128)S(1)} all-reduce(f32[128,8]{0,1:T(8,128)S(1)} %bitcast.78), channel_id=1, replica_groups=mesh['ctx'=32,'hg'=16] {'ctx'}, use_global_device_ids=true, to_apply=%region_6.7 | all-reduce | flops 1024 | bytes 8192 | tf_op jit(solution)/shard_map/pmax | solution.py:79
  240.0 2.1 bitcast_multiply_fusion
  242.1 55.7 %psum.15 = f32[128,8]{0,1:T(8,128)S(1)} all-reduce(f32[128,8]{0,1:T(8,128)S(1)} %get-tuple-element.225), channel_id=1, replica_groups=mesh['ctx'=32,'hg'=16] {'ctx'}, use_global_device_ids=true, to_apply=%region_8.9 | all-reduce | flops 1024 | bytes 8192 | tf_op jit(solution)/shard_map/psum | solution.py:81
  297.8 135.0 %all-reduce.3.cloned.1.call-done = f32[128,8,128]{2,0,1:T(8,128)} async-done(((f32[128,8,128]{2,0,1:T(8,128)}), f32[128,8,128]{2,0,1:T(8,128)}) %all-reduce.3.cloned.1.call-update) | async-done | bytes 524304 | tf_op jit(solution)/shard_map/psum | solution.py:81
  432.8 2.0 convolution_bitcast_fusion
  434.8 58.6 %reduce-scatter.2.cloned.1.call-done = f32[8,224]{1,0:T(8,128)} async-done(((f32[128,224]{1,0:T(8,128)}), f32[8,224]{1,0:T(8,128)}) %reduce-scatter.2.cloned.1.call-update) | async-done | bytes 7184 | tf_op jit(solution)/shard_map/reduce_scatter | solution.py:84
  493.4 1.3 convert_element_type.18
  (97 shorter events, 35.9 us)
Async XLA Ops:
  6.5 426.2 %copy-start = (bf16[8,128,224]{1,2,0:T(8,128)(2,1)S(1)}, bf16[8,128,224]{1,2,0:T(8,128)(2,1)}, u32[]{:S(2)}) copy-start(bf16[8,128,224]{1,2,0:T(8,128)(2,1)} %param.19) | copy-start | bytes 1376260
  6.5 426.2 %all-reduce.3.cloned.1.call-start = ((), (), s32[]{:S(2)}) async-start(), calls=%async_computation.1 | async-start | bytes 1048576 | tf_op jit(solution)/shard_map/psum | solution.py:81
  31.9 41.8 %copy-start.4 = (bf16[4,8,128]{2,1,0:T(8,128)(2,1)S(1)}, bf16[4,8,128]{2,1,0:T(8,128)(2,1)}, u32[]{:S(2)}) copy-start(bf16[4,8,128]{2,1,0:T(8,128)(2,1)} %param.13) | copy-start | bytes 24580
  31.9 77.3 %copy-start.5 = (bf16[4,8,64]{2,1,0:T(8,128)(2,1)S(1)}, bf16[4,8,64]{2,1,0:T(8,128)(2,1)}, u32[]{:S(2)}) copy-start(bf16[4,8,64]{2,1,0:T(8,128)(2,1)} %param.14) | copy-start | bytes 12292
  73.7 72.4 %copy-start.3 = (bf16[512,8,128]{2,1,0:T(8,128)(2,1)S(1)}, bf16[512,8,128]{2,1,0:T(8,128)(2,1)}, u32[]{:S(2)}) copy-start(bf16[512,8,128]{2,1,0:T(8,128)(2,1)} %param.18) | copy-start | bytes 3145732
  146.2 2.6 copy-start.1
  146.2 2.6 copy-start.2
  242.0 251.3 %reduce-scatter.2.cloned.1.call-start = ((), (), s32[]{:S(2)}) async-start(), calls=%async_computation.2 | async-start | bytes 139264 | tf_op jit(solution)/shard_map/reduce_scatter | solution.py:84
Sparse Core Ops, SparseCore 0:
  242.2 190.5 all-reduce.2
  435.8 57.5 reduce-scatter.1
where the time goes:
time: 504 us; the launch traced here: 502 us
  blocking collectives  208 us (41%)
  waiting for transfers between devices  194 us (38%)
  matrix products  31.9 us (6%)
  local copies, waits for them, and re-layouts  26.6 us (5%)
  loops' own time  21.1 us (4%)
  between operations  14.9 us (3%)
  other arithmetic  5.44 us (1%)
    psum x1, waiting for transfers between devices, per_device(): lax.psum((totals * rescale, output * rescale[:, :, None]), 'ctx')  135 us
    reduce_scatter x1, waiting for transfers between devices, per_device(): lax.psum_scatter(jnp.dot(attn, flat_weight, preferred_element_type=jnp.fl...  58.6 us
    pmax x1, blocking collectives, per_device(): overall = lax.pmax(maxima, 'ctx')  58.5 us
    psum x1, blocking collectives, per_device(): lax.psum((totals * rescale, output * rescale[:, :, None]), 'ctx')  55.7 us
    all_gather x1, blocking collectives, per_device(): lax.all_gather(query_rope, 'ctx', axis=0, tiled=True)  35.5 us
    all_gather x1, blocking collectives, per_device(): lax.all_gather(query_nope, 'ctx', axis=0, tiled=True)  35.4 us
    unnamed x1, blocking collectives  22.7 us
    another operation x1, loops' own time, prefix(): return lax.fori_loop(0, size, step, start)  21 us
  transfers between devices with their start and end apart: 2, of which 2 were waited for; matrix products, arithmetic and copies ran while one was open for 0% of the time, Pallas kernels for 0%

commit v1 on v0

v1 whole, which is shorter than its diff:
```python
import functools
import math

import jax
import jax.numpy as jnp
from jax import lax
from jax.experimental import pallas as pl
from jax.experimental.pallas import tpu as pltpu
from jax.sharding import PartitionSpec as P

NEG = -1e30
NCTX, NX, NZ, NHG = 32, 4, 8, 16
TOK, HD, DIM, ROPE, LAT, SLOTS, COLS = 128, 8, 128, 64, 512, 768, 224
FACTOR = 1.0 / math.sqrt(DIM + ROPE)
MESH = pl.DeviceIdType.MESH
F32, BF16 = jnp.float32, jnp.bfloat16


def rows(start, size, step=16):
    return pl.ds(pl.multiple_of(start, step), size)


def kernel(
    live, span, qn, qr, latent, rope_t, up_k, up_v, weight_t, out,
    lat_v, rope_v, upk_v, upv_v, wt_v, wide, wk, wvt, keys, values_t, kr,
    q_all, q_wide, o_mine, st_mine, o_all, st_all, a_all, part, part_all,
    load_sem, q_send, q_recv_z, q_recv_x, o_send, o_recv, st_send, st_recv,
    a_send, a_recv, p_send, p_recv,
):
    c, g = lax.axis_index("ctx"), lax.axis_index("hg")
    z = lax.rem(c, NZ)
    column = c - z

    def z_peer(k):
        return column + lax.rem(z + k, NZ)

    def x_peer(k):
        return lax.rem(c + NZ * k, NCTX)

    def h_peer(k):
        return lax.rem(g + k, NHG)

    def send(src, dst, send_sem, recv_sem, ctx, hg):
        pltpu.make_async_remote_copy(
            src_ref=src, dst_ref=dst, send_sem=send_sem, recv_sem=recv_sem,
            device_id=(ctx, hg), device_id_type=MESH,
        ).start()

    def drain(ref, sem):
        pltpu.make_async_copy(ref, ref, sem).wait()

    barrier = pltpu.get_barrier_semaphore()
    for k in range(1, NZ):
        pl.semaphore_signal(barrier, inc=1, device_id=(z_peer(k), g), device_id_type=MESH)
    for k in range(1, NX):
        pl.semaphore_signal(barrier, inc=1, device_id=(x_peer(k), g), device_id_type=MESH)
    for k in range(1, NHG):
        pl.semaphore_signal(barrier, inc=1, device_id=(c, h_peer(k)), device_id_type=MESH)

    loads = [
        pltpu.make_async_copy(src, dst, load_sem.at[i])
        for i, (src, dst) in enumerate(
            ((up_k, upk_v), (latent, lat_v), (up_v, upv_v), (rope_t, rope_v), (weight_t, wt_v))
        )
    ]
    for load in loads:
        load.start()

    count = live[0]
    nope = qn[...].astype(F32).reshape(4 * HD, DIM)
    rope = qr[...].astype(F32).reshape(4 * HD, ROPE)
    rope = jnp.concatenate([rope, jnp.zeros((4 * HD, DIM - ROPE), F32)], axis=1)
    lane = lax.broadcasted_iota(jnp.int32, (4 * HD, DIM), 1)
    high = lax.shift_right_logical(count, 3)
    low = count - high * 8
    rope = jnp.where(lane == ROPE, high.astype(F32), rope)
    rope = jnp.where(lane == ROPE + 1, low.astype(F32), rope)
    mine = rows(c * 32, 32)
    q_all[mine, 0:DIM] = nope.astype(BF16)
    q_all[mine, DIM:] = rope.astype(BF16)

    pl.semaphore_wait(barrier, (NZ - 1) + (NX - 1) + (NHG - 1))

    for k in (4, 3, 5, 2, 6, 1, 7):
        send(q_all.at[mine], q_all.at[mine], q_send, q_recv_z.at[k], z_peer(k), g)
    for j in (2, 1, 3):
        send(q_all.at[mine], q_all.at[mine], q_send, q_recv_x, x_peer(j), g)

    loads[0].wait()
    wide[...] = upk_v[...].astype(F32).reshape(LAT * HD, DIM)
    for h in range(HD):
        wk[:, h * DIM : (h + 1) * DIM] = wide[pl.ds(h, LAT, stride=HD), :].astype(BF16)
    loads[1].wait()
    for h in range(0, HD, 2):
        both = jnp.dot(
            lat_v[...], wk[:, h * DIM : (h + 2) * DIM], preferred_element_type=F32
        ).astype(BF16)
        keys[h] = both[:, 0:DIM]
        keys[h + 1] = both[:, DIM:]

    for k in (1, 7, 2, 6, 3, 5, 4):
        block = rows(z_peer(k) * 32, 32)
        drain(q_all.at[block], q_recv_z.at[NZ - k])
        for j in (2, 1, 3):
            send(q_all.at[block], q_all.at[block], q_send, q_recv_x, x_peer(j), g)

    loads[2].wait()
    wide[...] = upv_v[...].astype(F32).reshape(LAT * HD, DIM)
    for h in range(HD):
        wvt[h * DIM : (h + 1) * DIM, :] = wide[pl.ds(h, LAT, stride=HD), :].T.astype(BF16)
    for n in range(0, SLOTS, 256):
        values_t[:, n : n + 256] = lax.dot_general(
            wvt[...], lat_v[n : n + 256, :], (((1,), (1,)), ((), ())),
            preferred_element_type=F32,
        ).astype(BF16)
    loads[3].wait()
    kr[...] = jnp.concatenate(
        [rope_v[...].astype(F32), jnp.zeros((DIM - ROPE, SLOTS), F32)], axis=0
    ).T.astype(BF16)

    drain(q_all.at[pl.ds(0, 24 * 32)], q_recv_x)
    q_wide[0] = q_all[:, 0:DIM].astype(F32)
    q_wide[1] = q_all[:, DIM:].astype(F32)
    counts = q_wide[1, pl.ds(0, NCTX, stride=32), :]
    lane = lax.broadcasted_iota(jnp.int32, (NCTX, DIM), 1)
    shard = lax.broadcasted_iota(jnp.int32, (NCTX, DIM), 0)
    scale = jnp.where(lane == ROPE, 8.0, jnp.where(lane == ROPE + 1, 1.0, 0.0))
    before = jnp.where(shard < c, counts * scale, 0.0)
    offset = jnp.sum(jnp.sum(before, axis=0, keepdims=True), axis=1, keepdims=True)
    offset = offset.astype(jnp.int32)
    token = lax.broadcasted_iota(jnp.int32, (1, TOK), 1)
    limit = jnp.minimum(token + (span[0] + 1) - offset, count)
    slot = lax.broadcasted_iota(jnp.int32, (SLOTS, TOK), 0)
    visible = slot < limit

    own = lax.div(c, 4)
    for t in range(HD):
        h = lax.rem(own + 1 + t, HD)
        q = jnp.concatenate(
            [q_wide[i, pl.ds(h, TOK, stride=HD), :].astype(BF16) for i in range(2)], axis=1
        )
        k_cat = jnp.concatenate([keys[h], kr[...]], axis=1)
        scores = lax.dot_general(
            k_cat, q, (((1,), (1,)), ((), ())), preferred_element_type=F32
        )
        scores = jnp.where(visible, scores, NEG)
        top = jnp.max(scores, axis=0, keepdims=True)
        p = jnp.exp((scores - top) * FACTOR)
        st_mine[h, 0:1, :] = top
        st_mine[h, 1:2, :] = jnp.sum(p, axis=0, keepdims=True)
        feats = rows(h * DIM, DIM, DIM)
        o_mine[feats, :] = jnp.dot(
            values_t[feats, :], p.astype(BF16), preferred_element_type=F32
        ).astype(BF16)
        for j in range(4) if t < HD - 1 else range(1, 4):
            dst = 4 * h + (j if t < HD - 1 else lax.rem(c + j, 4))
            place = lax.rem(c - dst + NCTX, NCTX)
            send(
                o_mine.at[rows(dst * 32, 32)], o_all.at[rows(place * 32, 32)],
                o_send, o_recv, dst, g,
            )
            send(st_mine.at[h], st_all.at[place], st_send, st_recv, dst, g)

    o_all[0:32, :] = o_mine[mine, :]
    st_all[0] = st_mine[own]
    drain(st_all.at[pl.ds(1, NCTX - 1)], st_recv)
    drain(o_all.at[pl.ds(32, (NCTX - 1) * 32)], o_recv)
    tops = st_all[:, 0, :]
    weights = jnp.exp((tops - jnp.max(tops, axis=0, keepdims=True)) * FACTOR)
    total = jnp.sum(weights * st_all[:, 1, :], axis=0, keepdims=True)
    joined = jnp.zeros((32, TOK), F32)
    for s in range(NCTX):
        joined = joined + o_all[s * 32 : (s + 1) * 32, :].astype(F32) * weights[s : s + 1, :]
    a_all[mine, :] = (joined / total).astype(BF16)
    for k in range(1, NCTX):
        send(a_all.at[mine], a_all.at[mine], a_send, a_recv, lax.rem(c + k, NCTX), g)

    loads[4].wait()
    w = jnp.concatenate([wt_v[h] for h in range(HD)], axis=1)
    drain(a_all.at[pl.ds(0, (NCTX - 1) * 32)], a_recv)
    mixed_t = jnp.dot(w, a_all[...], preferred_element_type=F32)
    mixed_t = jnp.concatenate([mixed_t, jnp.zeros((256 - COLS, TOK), F32)], axis=0)
    left = mixed_t[0:128].T.reshape(NHG, 8, 128)
    right = mixed_t[128:].T.reshape(NHG, 8, 128)
    part[...] = jnp.concatenate([left, right], axis=1).astype(BF16).reshape(NHG * 16, 128)
    for k in range(1, NHG):
        send(
            part.at[rows(h_peer(k) * 16, 16)], part_all.at[pl.ds((NHG - k) * 16, 16)],
            p_send, p_recv, c, h_peer(k),
        )
    acc = part[rows(g * 16, 16), :].astype(F32)
    drain(part_all.at[pl.ds(16, (NHG - 1) * 16)], p_recv)
    for k in range(1, NHG):
        acc = acc + part_all[k * 16 : (k + 1) * 16, :].astype(F32)
    out[...] = jnp.concatenate([acc[0:8], acc[8:16, 0 : COLS - 128]], axis=1).astype(BF16)

    drain(q_all.at[pl.ds(0, 31 * 32)], q_send)
    drain(o_all.at[pl.ds(32, (NCTX - 1) * 32)], o_send)
    drain(st_all.at[pl.ds(1, NCTX - 1)], st_send)
    drain(a_all.at[pl.ds(0, (NCTX - 1) * 32)], a_send)
    drain(part_all.at[pl.ds(16, (NHG - 1) * 16)], p_send)


def per_device(
    query_nope, query_rope, latent, key_rope, up_keys, up_values, out_weight, live_rows, span_start
):
    anywhere = pl.BlockSpec(memory_space=pl.ANY)
    vmem = pl.BlockSpec(memory_space=pltpu.VMEM)
    smem = pl.BlockSpec(memory_space=pltpu.SMEM)
    dma = pltpu.SemaphoreType.DMA
    return pl.pallas_call(
        kernel,
        out_shape=jax.ShapeDtypeStruct((TOK // NHG, COLS), BF16),
        in_specs=[smem, smem, vmem, vmem] + [anywhere] * 5,
        out_specs=vmem,
        scratch_shapes=[
            pltpu.VMEM((SLOTS, LAT), BF16),
            pltpu.VMEM((ROPE, SLOTS), BF16),
            pltpu.VMEM((LAT, HD, DIM), BF16),
            pltpu.VMEM((LAT, HD, DIM), BF16),
            pltpu.VMEM((HD, COLS, DIM), BF16),
            pltpu.VMEM((LAT * HD, DIM), F32),
            pltpu.VMEM((LAT, HD * DIM), BF16),
            pltpu.VMEM((HD * DIM, LAT), BF16),
            pltpu.VMEM((HD, SLOTS, DIM), BF16),
            pltpu.VMEM((HD * DIM, SLOTS), BF16),
            pltpu.VMEM((SLOTS, DIM), BF16),
            pltpu.VMEM((TOK * HD, 2 * DIM), BF16),
            pltpu.VMEM((2, TOK * HD, DIM), F32),
            pltpu.VMEM((HD * DIM, TOK), BF16),
            pltpu.VMEM((HD, 2, TOK), F32),
            pltpu.VMEM((NCTX * 32, TOK), BF16),
            pltpu.VMEM((NCTX, 2, TOK), F32),
            pltpu.VMEM((HD * DIM, TOK), BF16),
            pltpu.VMEM((NHG * 16, 128), BF16),
            pltpu.VMEM((NHG * 16, 128), BF16),
            dma((5,)), dma, dma((NZ,)), dma, dma, dma, dma, dma, dma, dma, dma, dma,
        ],
        compiler_params=pltpu.CompilerParams(
            collective_id=0, has_side_effects=True, vmem_limit_bytes=48 * 1024 * 1024
        ),
    )(
        live_rows, span_start, query_nope, query_rope, latent, key_rope.T, up_keys, up_values,
        jnp.transpose(out_weight, (0, 2, 1)),
    )


def solution(mesh):
    placed = (
        P("ctx", "hg", None),
        P("ctx", "hg", None),
        P("ctx", None),
        P("ctx", None),
        P(None, "hg", None),
        P(None, "hg", None),
        P("hg", None, "ctx"),
        P("ctx"),
        P(),
    )
    return jax.shard_map(
        per_device, mesh=mesh, in_specs=placed, out_specs=P("hg", "ctx"), check_vma=False
    )
```

time: 504 us -> 59.8 us (0.12)
  blocking collectives: 208 us -> 0 us
  waiting for transfers between devices: 194 us -> 0 us
  Pallas kernels: 0 us -> 50.6 us
  matrix products: 31.9 us -> 0 us
  loops' own time: 21.1 us -> 0 us
  local copies, waits for them, and re-layouts: 26.6 us -> 7.47 us
  between operations: 14.9 us -> 1.32 us
  other arithmetic: 5.44 us -> 0 us
    psum x1 -> x0, waiting for transfers between devices: 135 us -> none  [per_device(): lax.psum((totals * rescale, output * rescale[:, :, None]), 'ctx')]
    all_gather x2 -> x0, blocking collectives: 70.9 us -> none  [the longest x1 35.5 us: per_device(): lax.all_gather(query_rope, 'ctx', axis=0, tiled=True)]
    reduce_scatter x1 -> x0, waiting for transfers between devices: 58.6 us -> none  [per_device(): lax.psum_scatter(jnp.dot(attn, flat_weight, preferred_element_type=jnp.fl...]
    pmax x1 -> x0, blocking collectives: 58.5 us -> none  [per_device(): overall = lax.pmax(maxima, 'ctx')]
    psum x1 -> x0, blocking collectives: 55.7 us -> none  [per_device(): lax.psum((totals * rescale, output * rescale[:, :, None]), 'ctx')]
    pallas_call x0 -> x1, Pallas kernels: none -> 50.6 us  [per_device(): pl.pallas_call(kernel, out_shape=jax.ShapeDtypeStruct((TOK // NHG, COLS),...]
    dot_general x25 -> x0, matrix products: 31.9 us -> none  [the longest x8 16.9 us: one_head(): jnp.dot(weights.astype(jnp.bfloat16), values_one, preferred_element_type=...]
    unnamed x1 -> x0, blocking collectives: 22.7 us -> none
  transfers between devices with their start and end apart: 2 -> 0, of which waited for: 2 -> 0; matrix products, arithmetic and copies ran while one was open for 0% -> 0% of each run, Pallas kernels for 0% -> 0%
where the time goes in v1:
time: 59.8 us; the launch traced here: 59.4 us
  Pallas kernels  50.6 us (85%)
  local copies, waits for them, and re-layouts  7.47 us (12%)
  between operations  1.32 us (2%)
    pallas_call x1, Pallas kernels, per_device(): pl.pallas_call(kernel, out_shape=jax.ShapeDtypeStruct((TOK // NHG, COLS),...  50.6 us
    unnamed x15, local copies, waits for them, and re-layouts  7.47 us

profile of v1, /device:TPU:1, one launch (start us, length us, event | category | flops | bytes accessed | tf_op | source)
XLA Modules:
  0.0 59.4 jit_solution(4431893263249853804)
XLA Ops:
  1.3 0.0 copy-start
  1.3 1.2 %copy-done = bf16[512,8,128]{2,1,0:T(8,128)(2,1)S(1)} copy-done((bf16[512,8,128]{2,1,0:T(8,128)(2,1)S(1)}, bf16[512,8,128]{2,1,0:T(8,128)(2,1)}, u32[]{:S(2)}) %copy-start) | copy-done | bytes 1048600
  2.5 0.0 copy-start.1
  2.5 1.2 %copy-done.1 = bf16[512,8,128]{2,1,0:T(8,128)(2,1)S(1)} copy-done((bf16[512,8,128]{2,1,0:T(8,128)(2,1)S(1)}, bf16[512,8,128]{2,1,0:T(8,128)(2,1)}, u32[]{:S(2)}) %copy-start.1) | copy-done | bytes 1048600
  3.7 0.0 copy-start.2
  3.8 1.1 %copy-done.2 = bf16[768,512]{1,0:T(8,128)(2,1)S(1)} copy-done((bf16[768,512]{1,0:T(8,128)(2,1)S(1)}, bf16[768,512]{1,0:T(8,128)(2,1)}, u32[]{:S(2)}) %copy-start.2) | copy-done | bytes 786456
  4.9 0.0 copy-start.3
  4.9 1.0 %copy-done.3 = bf16[8,128,224]{1,2,0:T(8,128)(2,1)S(1)} copy-done((bf16[8,128,224]{1,2,0:T(8,128)(2,1)S(1)}, bf16[8,128,224]{1,2,0:T(8,128)(2,1)}, u32[]{:S(2)}) %copy-start.3) | copy-done | bytes 458776
  5.9 0.0 copy-start.4
  5.9 0.9 %copy-done.4 = bf16[768,64]{0,1:T(8,128)(2,1)S(1)} copy-done((bf16[768,64]{0,1:T(8,128)(2,1)S(1)}, bf16[768,64]{0,1:T(8,128)(2,1)}, u32[]{:S(2)}) %copy-start.4) | copy-done | bytes 98328
  6.8 0.0 copy-start.5
  6.8 0.7 %copy-done.5 = bf16[4,8,128]{2,1,0:T(8,128)(2,1)S(1)} copy-done((bf16[4,8,128]{2,1,0:T(8,128)(2,1)S(1)}, bf16[4,8,128]{2,1,0:T(8,128)(2,1)}, u32[]{:S(2)}) %copy-start.5) | copy-done | bytes 8216
  7.5 0.0 copy-start.6
  7.5 0.7 %copy-done.6 = bf16[4,8,64]{2,1,0:T(8,128)(2,1)S(1)} copy-done((bf16[4,8,64]{2,1,0:T(8,128)(2,1)S(1)}, bf16[4,8,64]{2,1,0:T(8,128)(2,1)}, u32[]{:S(2)}) %copy-start.6) | copy-done | bytes 4120
  8.2 50.6 %shard_map.91 = bf16[8,224]{1,0:T(8,128)(2,1)S(1)} custom-call(s32[1]{0:T(128)S(6)} %copy.11.live, s32[1]{0:T(128)S(6)} %copy.12.span, bf16[4,8,128]{2,1,0:T(8,128)(2,1)S(1)} %copy-done.5, bf16[4,8,64]{2,1,0:T(8,128)(2,1)S(1)} %copy-done.6, bf16[768,512]{1,0:T(8,128)(2,1)S(1)} %copy-done.2, bf16[64,768]{1,0:T(8,128)(2,1)S(1)} %bitcast.3, ...), custom_call_target="tpu_custom_call" | custom-call | tf_op jit(solution)/shard_map/pallas_call | solution.py:211
  58.8 0.6 %copy.13 = bf16[8,224]{1,0:T(8,128)(2,1)} copy(bf16[8,224]{1,0:T(8,128)(2,1)S(1)} %shard_map.91) | data formatting | bytes 7168
Async XLA Ops:
  1.3 1.2 %copy-start = (bf16[512,8,128]{2,1,0:T(8,128)(2,1)S(1)}, bf16[512,8,128]{2,1,0:T(8,128)(2,1)}, u32[]{:S(2)}) copy-start(bf16[512,8,128]{2,1,0:T(8,128)(2,1)} %up_k.1) | copy-start | bytes 3145732
  2.5 1.2 %copy-start.1 = (bf16[512,8,128]{2,1,0:T(8,128)(2,1)S(1)}, bf16[512,8,128]{2,1,0:T(8,128)(2,1)}, u32[]{:S(2)}) copy-start(bf16[512,8,128]{2,1,0:T(8,128)(2,1)} %up_v.1) | copy-start | bytes 3145732
  3.7 1.1 %copy-start.2 = (bf16[768,512]{1,0:T(8,128)(2,1)S(1)}, bf16[768,512]{1,0:T(8,128)(2,1)}, u32[]{:S(2)}) copy-start(bf16[768,512]{1,0:T(8,128)(2,1)} %latent.1) | copy-start | bytes 2359300
  4.9 1.0 %copy-start.3 = (bf16[8,128,224]{1,2,0:T(8,128)(2,1)S(1)}, bf16[8,128,224]{1,2,0:T(8,128)(2,1)}, u32[]{:S(2)}) copy-start(bf16[8,128,224]{1,2,0:T(8,128)(2,1)} %param.15) | copy-start | bytes 1376260
  5.9 0.9 %copy-start.4 = (bf16[768,64]{0,1:T(8,128)(2,1)S(1)}, bf16[768,64]{0,1:T(8,128)(2,1)}, u32[]{:S(2)}) copy-start(bf16[768,64]{0,1:T(8,128)(2,1)} %param.12) | copy-start | bytes 294916
  6.8 0.7 %copy-start.5 = (bf16[4,8,128]{2,1,0:T(8,128)(2,1)S(1)}, bf16[4,8,128]{2,1,0:T(8,128)(2,1)}, u32[]{:S(2)}) copy-start(bf16[4,8,128]{2,1,0:T(8,128)(2,1)} %qn.1) | copy-start | bytes 24580
  7.5 0.7 %copy-start.6 = (bf16[4,8,64]{2,1,0:T(8,128)(2,1)S(1)}, bf16[4,8,64]{2,1,0:T(8,128)(2,1)}, u32[]{:S(2)}) copy-start(bf16[4,8,64]{2,1,0:T(8,128)(2,1)} %qr.1) | copy-start | bytes 12292

commit v2 on v1

v2 whole, which is shorter than its diff:
```python
import math

import jax
import jax.numpy as jnp
from jax import lax
from jax.experimental import pallas as pl
from jax.experimental.pallas import tpu as pltpu
from jax.sharding import PartitionSpec as P

NEG = -1e30
NCTX, NX, NZ, NHG = 32, 4, 8, 16
TOK, HD, DIM, ROPE, LAT, SLOTS, COLS = 128, 8, 128, 64, 512, 768, 224
PAIRS = HD // 2
FACTOR = 1.0 / math.sqrt(DIM + ROPE)
MESH = pl.DeviceIdType.MESH
F32, BF16 = jnp.float32, jnp.bfloat16
NEAR_FIRST = (1, 7, 2, 6, 3, 5, 4)
FAR_FIRST = (4, 3, 5, 2, 6, 1, 7)


def rows(start, size):
    return pl.ds(pl.multiple_of(start, size), size)


def kernel(
    live_h, span_h, qn_h, qr_h, latent, rope_t, up_k, up_v, weight_t, out,
    live, span, qn, qr, lat_v, rope_v, upk_v, upv_v, wt_v, small, wide, wk, wvt,
    keys, values_t, kr, qa_all, qb_all, q_wide, r_wide, counts,
    o_mine, lse_mine, o_all, lse_all, a_all, part, part_all,
    load_sem, q_send, qz_recv, qx_recv, n_send, nz_recv, nx_recv,
    o_send, o_recv, lse_send, lse_recv, a_send, az_recv, ax_recv, ab_recv, p_send, p_recv,
):
    c, g = lax.axis_index("ctx"), lax.axis_index("hg")
    z, x = lax.rem(c, NZ), lax.div(c, NZ)
    column = x * NZ

    def z_peer(k):
        return column + lax.rem(z + k, NZ)

    def x_peer(k):
        return lax.rem(c + NZ * k, NCTX)

    def h_peer(k):
        return lax.rem(g + k, NHG)

    def send(src, dst, send_sem, recv_sem, ctx, hg):
        pltpu.make_async_remote_copy(
            src_ref=src, dst_ref=dst, send_sem=send_sem, recv_sem=recv_sem,
            device_id=(ctx, hg), device_id_type=MESH,
        ).start()

    def drain(ref, sem):
        pltpu.make_async_copy(ref, ref, sem).wait()

    barrier = pltpu.get_barrier_semaphore()
    for k in range(1, NZ):
        pl.semaphore_signal(barrier, inc=1, device_id=(z_peer(k), g), device_id_type=MESH)
    for k in range(1, NX):
        pl.semaphore_signal(barrier, inc=1, device_id=(x_peer(k), g), device_id_type=MESH)
    for k in range(1, NHG):
        pl.semaphore_signal(barrier, inc=1, device_id=(c, h_peer(k)), device_id_type=MESH)

    loads = [
        pltpu.make_async_copy(src, dst, load_sem.at[i])
        for i, (src, dst) in enumerate(
            (
                (live_h, live), (span_h, span), (qn_h, qn), (qr_h, qr),
                (up_k, upk_v), (latent, lat_v), (up_v, upv_v), (rope_t, rope_v), (weight_t, wt_v),
            )
        )
    ]
    for load in loads:
        load.start()
    for load in loads[:4]:
        load.wait()

    count = live[0]
    small[0] = qn[...].astype(F32).reshape(4 * HD, DIM)
    rope = qr[...].astype(F32).reshape(4 * HD, ROPE)
    small[1] = jnp.concatenate([rope, rope], axis=1)
    even, odd = pl.ds(0, 16, stride=2), pl.ds(1, 16, stride=2)
    lane = lax.broadcasted_iota(jnp.int32, (16, DIM), 1)
    mine16, mine32 = rows(c * 16, 16), rows(c * 32, 32)
    both = jnp.where(lane < ROPE, small[1, even, :], small[1, odd, :])
    qa_all[mine32, :] = jnp.concatenate([small[0, even, :], both], axis=0).astype(BF16)
    qb_all[mine16, :] = small[0, odd, :].astype(BF16)
    counts[c] = jnp.zeros((1, DIM), F32) + count.astype(F32)

    pl.semaphore_wait(barrier, (NZ - 1) + (NX - 1) + (NHG - 1))

    q_parts = ((qa_all, 32), (qb_all, 16))
    for i, (ref, size) in enumerate(q_parts):
        block = ref.at[rows(c * size, size)]
        for k in FAR_FIRST:
            send(block, block, q_send.at[i], qz_recv.at[i, k], z_peer(k), g)
            if i == 0:
                send(counts.at[c], counts.at[c], n_send, nz_recv, z_peer(k), g)
        for j in (2, 1, 3):
            send(block, block, q_send.at[i], qx_recv.at[i], x_peer(j), g)

    loads[4].wait()
    wide[...] = upk_v[...].astype(F32).reshape(LAT * HD, DIM)
    for h in range(HD):
        wk[:, h * DIM : (h + 1) * DIM] = wide[pl.ds(h, LAT, stride=HD), :].astype(BF16)
    loads[5].wait()
    for h in range(0, HD, 2):
        two = jnp.dot(
            lat_v[...], wk[:, h * DIM : (h + 2) * DIM], preferred_element_type=F32
        ).astype(BF16)
        keys[h] = two[:, 0:DIM]
        keys[h + 1] = two[:, DIM:]

    loads[6].wait()
    wide[...] = upv_v[...].astype(F32).reshape(LAT * HD, DIM)
    for h in range(HD):
        wvt[h * DIM : (h + 1) * DIM, :] = wide[pl.ds(h, LAT, stride=HD), :].T.astype(BF16)
    for n in range(0, SLOTS, 256):
        values_t[:, n : n + 256] = lax.dot_general(
            wvt[...], lat_v[n : n + 256, :], (((1,), (1,)), ((), ())),
            preferred_element_type=F32,
        ).astype(BF16)
    loads[7].wait()
    rope = rope_v[...].astype(F32)
    blank = jnp.zeros((DIM - ROPE, SLOTS), F32)
    kr[0] = jnp.concatenate([rope, blank], axis=0).T.astype(BF16)
    kr[1] = jnp.concatenate([blank, rope], axis=0).T.astype(BF16)

    for i, (ref, size) in enumerate(q_parts):
        for k in NEAR_FIRST:
            block = ref.at[rows(z_peer(k) * size, size)]
            drain(block, qz_recv.at[i, NZ - k])
            for j in (2, 1, 3):
                send(block, block, q_send.at[i], qx_recv.at[i], x_peer(j), g)
        if i == 0:
            drain(counts.at[pl.ds(0, NZ - 1)], nz_recv)
            some = counts.at[rows(column, NZ)]
            for j in (2, 1, 3):
                send(some, some, n_send, nx_recv, x_peer(j), g)

    drain(counts.at[pl.ds(0, 24)], nx_recv)
    shard = lax.broadcasted_iota(jnp.int32, (NCTX, DIM), 0)
    before = jnp.where(shard < c, counts[:, 0, :], 0.0)
    offset = jnp.sum(before, axis=0, keepdims=True).astype(jnp.int32)
    token = lax.broadcasted_iota(jnp.int32, (1, TOK), 1)
    limit = jnp.minimum(token + (span[0] + 1) - offset, count)
    slot = lax.broadcasted_iota(jnp.int32, (SLOTS, TOK), 0)

    for i, (ref, size) in enumerate(q_parts):
        drain(ref.at[pl.ds(0, 24 * size)], qx_recv.at[i])
        got = ref[...].astype(F32).reshape(NCTX, size, DIM)
        q_wide[...] = got[:, 0:16].reshape(NCTX * 16, DIM)
        if i == 0:
            r_wide[...] = got[:, 16:32].reshape(NCTX * 16, DIM)
        for t in range(PAIRS):
            p = lax.rem(x + 1 + t, NX)
            h = 2 * p + i
            mine = pl.ds(p, TOK, stride=PAIRS)
            q = jnp.concatenate(
                [q_wide[mine, :].astype(BF16), r_wide[mine, :].astype(BF16)], axis=1
            )
            k_cat = jnp.concatenate([keys[h], kr[i]], axis=1)
            scores = lax.dot_general(
                k_cat, q, (((1,), (1,)), ((), ())), preferred_element_type=F32
            )
            scores = jnp.where(slot < limit, scores, NEG)
            top = jnp.max(scores, axis=0, keepdims=True)
            weights = jnp.exp((scores - top) * FACTOR)
            total = jnp.sum(weights, axis=0, keepdims=True)
            lse_mine[i, p] = top * FACTOR + jnp.log(total)
            summed = jnp.dot(
                values_t[rows(h * DIM, DIM), :], weights.astype(BF16), preferred_element_type=F32
            )
            o_mine[i, rows(p * DIM, DIM), :] = (summed / total).astype(BF16)
            for j in (4, 3, 5, 2, 6, 1, 7, 0):
                if t == PAIRS - 1 and j == 0:
                    continue
                dst = p * NZ + lax.rem(z + j, NZ)
                place = lax.rem(c - dst + NCTX, NCTX)
                send(
                    lse_mine.at[i, p], lse_all.at[i, place], lse_send.at[i], lse_recv.at[i], dst, g
                )
                send(
                    o_mine.at[i, rows(dst * 16, 16)], o_all.at[i, rows(place * 16, 16)],
                    o_send.at[i], o_recv.at[i], dst, g,
                )

    for i in range(2):
        o_all[i, 0:16, :] = o_mine[i, mine16, :]
        lse_all[i, 0] = lse_mine[i, x]
        drain(lse_all.at[i, pl.ds(1, NCTX - 1)], lse_recv.at[i])
        lse = lse_all[i, :, 0, :]
        share = jnp.exp(lse - jnp.max(lse, axis=0, keepdims=True))
        share = share / jnp.sum(share, axis=0, keepdims=True)
        drain(o_all.at[i, pl.ds(16, (NCTX - 1) * 16)], o_recv.at[i])
        joined = jnp.zeros((16, TOK), F32)
        for s in range(NCTX):
            joined = joined + o_all[i, s * 16 : (s + 1) * 16, :].astype(F32) * share[s : s + 1, :]
        a_all[i, mine16, :] = joined.astype(BF16)
        block = a_all.at[i, mine16]
        if i == 0:
            for k in FAR_FIRST:
                send(block, block, a_send.at[i], az_recv.at[k], z_peer(k), g)
            for j in (2, 1, 3):
                send(block, block, a_send.at[i], ax_recv, x_peer(j), g)
        else:
            for k in FAR_FIRST + (0,):
                for j in (2, 1, 3, 0):
                    if k or j:
                        dst = lax.rem(z_peer(k) + NZ * j, NCTX)
                        send(block, block, a_send.at[i], ab_recv, dst, g)
    for k in NEAR_FIRST:
        block = a_all.at[0, rows(z_peer(k) * 16, 16)]
        drain(block, az_recv.at[NZ - k])
        for j in (2, 1, 3):
            send(block, block, a_send.at[0], ax_recv, x_peer(j), g)

    loads[8].wait()
    w = [jnp.concatenate([wt_v[2 * p + i] for p in range(PAIRS)], axis=1) for i in range(2)]
    drain(a_all.at[0, pl.ds(0, 24 * 16)], ax_recv)
    mixed_t = jnp.dot(w[0], a_all[0], preferred_element_type=F32)
    drain(a_all.at[1, pl.ds(0, (NCTX - 1) * 16)], ab_recv)
    mixed_t = mixed_t + jnp.dot(w[1], a_all[1], preferred_element_type=F32)
    mixed_t = jnp.concatenate([mixed_t, jnp.zeros((256 - COLS, TOK), F32)], axis=0)
    left = mixed_t[0:128].T.reshape(NHG, 8, 128)
    right = mixed_t[128:].T.reshape(NHG, 8, 128)
    part[...] = jnp.concatenate([left, right], axis=1).astype(BF16).reshape(NHG * 16, 128)
    for k in (8, 9, 7, 10, 6, 11, 5, 12, 4, 13, 3, 14, 2, 15, 1):
        send(
            part.at[rows(h_peer(k) * 16, 16)], part_all.at[pl.ds((NHG - k) * 16, 16)],
            p_send, p_recv, c, h_peer(k),
        )
    acc = part[rows(g * 16, 16), :].astype(F32)
    drain(part_all.at[pl.ds(16, (NHG - 1) * 16)], p_recv)
    for k in range(1, NHG):
        acc = acc + part_all[k * 16 : (k + 1) * 16, :].astype(F32)
    out[...] = jnp.concatenate([acc[0:8], acc[8:16, 0 : COLS - 128]], axis=1).astype(BF16)

    for i, (ref, size) in enumerate(q_parts):
        drain(ref.at[pl.ds(0, 31 * size)], q_send.at[i])
        drain(o_all.at[i, pl.ds(16, (NCTX - 1) * 16)], o_send.at[i])
        drain(lse_all.at[i, pl.ds(1, NCTX - 1)], lse_send.at[i])
        drain(a_all.at[i, pl.ds(0, (NCTX - 1) * 16)], a_send.at[i])
    drain(counts.at[pl.ds(0, 31)], n_send)
    drain(part_all.at[pl.ds(16, (NHG - 1) * 16)], p_send)


def per_device(
    query_nope, query_rope, latent, key_rope, up_keys, up_values, out_weight, live_rows, span_start
):
    hbm = pl.BlockSpec(memory_space=pltpu.HBM)
    dma = pltpu.SemaphoreType.DMA
    call = pl.pallas_call(
        kernel,
        out_shape=jax.ShapeDtypeStruct((TOK // NHG, COLS), BF16),
        in_specs=[hbm] * 9,
        out_specs=pl.BlockSpec(memory_space=pltpu.VMEM),
        scratch_shapes=[
            pltpu.SMEM((1,), jnp.int32),
            pltpu.SMEM((1,), jnp.int32),
            pltpu.VMEM((4, HD, DIM), BF16),
            pltpu.VMEM((4, HD, ROPE), BF16),
            pltpu.VMEM((SLOTS, LAT), BF16),
            pltpu.VMEM((ROPE, SLOTS), BF16),
            pltpu.VMEM((LAT, HD, DIM), BF16),
            pltpu.VMEM((LAT, HD, DIM), BF16),
            pltpu.VMEM((HD, COLS, DIM), BF16),
            pltpu.VMEM((2, 4 * HD, DIM), F32),
            pltpu.VMEM((LAT * HD, DIM), F32),
            pltpu.VMEM((LAT, HD * DIM), BF16),
            pltpu.VMEM((HD * DIM, LAT), BF16),
            pltpu.VMEM((HD, SLOTS, DIM), BF16),
            pltpu.VMEM((HD * DIM, SLOTS), BF16),
            pltpu.VMEM((2, SLOTS, DIM), BF16),
            pltpu.VMEM((NCTX * 32, DIM), BF16),
            pltpu.VMEM((NCTX * 16, DIM), BF16),
            pltpu.VMEM((NCTX * 16, DIM), F32),
            pltpu.VMEM((NCTX * 16, DIM), F32),
            pltpu.VMEM((NCTX, 1, DIM), F32),
            pltpu.VMEM((2, PAIRS * DIM, TOK), BF16),
            pltpu.VMEM((2, PAIRS, 1, TOK), F32),
            pltpu.VMEM((2, NCTX * 16, TOK), BF16),
            pltpu.VMEM((2, NCTX, 1, TOK), F32),
            pltpu.VMEM((2, PAIRS * DIM, TOK), BF16),
            pltpu.VMEM((NHG * 16, 128), BF16),
            pltpu.VMEM((NHG * 16, 128), BF16),
            dma((9,)), dma((2,)), dma((2, NZ)), dma((2,)), dma, dma, dma,
            dma((2,)), dma((2,)), dma((2,)), dma((2,)), dma((2,)), dma((NZ,)), dma, dma, dma, dma,
        ],
        compiler_params=pltpu.CompilerParams(
            collective_id=0, has_side_effects=True, vmem_limit_bytes=48 * 1024 * 1024
        ),
    )
    large = (
        query_nope, query_rope, latent, key_rope.T, up_keys, up_values,
        jnp.transpose(out_weight, (0, 2, 1)),
    )
    return call(
        live_rows, span_start, *[pltpu.with_memory_space_constraint(a, pltpu.HBM) for a in large]
    )


def solution(mesh):
    placed = (
        P("ctx", "hg", None),
        P("ctx", "hg", None),
        P("ctx", None),
        P("ctx", None),
        P(None, "hg", None),
        P(None, "hg", None),
        P("hg", None, "ctx"),
        P("ctx"),
        P(),
    )
    return jax.shard_map(
        per_device, mesh=mesh, in_specs=placed, out_specs=P("hg", "ctx"), check_vma=False
    )
```

time: 59.8 us -> 48.7 us (0.81)
  local copies, waits for them, and re-layouts: 7.47 us -> 0.6 us
  Pallas kernels: 50.6 us -> 46.7 us
    unnamed x15 -> x1, local copies, waits for them, and re-layouts: 7.47 us -> 0.6 us
    pallas_call x1, Pallas kernels: 50.6 us -> 46.7 us  [per_device(): call(live_rows, span_start, *[pltpu.with_memory_space_constraint(a, pltpu...]
where the time goes in v2:
time: 48.7 us; the launch traced here: 48.6 us
  Pallas kernels  46.7 us (96%)
  between operations  1.3 us (3%)
  local copies, waits for them, and re-layouts  0.6 us (1%)
    pallas_call x1, Pallas kernels, per_device(): call(live_rows, span_start, *[pltpu.with_memory_space_constraint(a, pltpu...  46.7 us

profile of v2, /device:TPU:1, one launch (start us, length us, event | category | flops | bytes accessed | tf_op | source)
XLA Modules:
  0.0 48.6 jit_solution(1682119367635260509)
XLA Ops:
  1.3 46.7 %shard_map.91 = bf16[8,224]{1,0:T(8,128)(2,1)S(1)} custom-call(s32[1]{0:T(128)S(6)} %copy.11.live_h, s32[1]{0:T(128)S(6)} %copy.12.span_h, bf16[4,8,128]{2,1,0:T(8,128)(2,1)} %qn_h.1, bf16[4,8,64]{2,1,0:T(8,128)(2,1)} %qr_h.1, bf16[768,512]{1,0:T(8,128)(2,1)} %latent.1, bf16[64,768]{1,0:T(8,128)(2,1)} %bitcast.3, bf16[512,8,128]{2,1,0:T(8,128)(2,1)} %up_k.1, ...), custom_call_target="tpu_custom_call" | custom-call | tf_op jit(solution)/shard_map/pallas_call | solution.py:297
  48.0 0.6 %copy.13 = bf16[8,224]{1,0:T(8,128)(2,1)} copy(bf16[8,224]{1,0:T(8,128)(2,1)S(1)} %shard_map.91) | data formatting | bytes 7168

commit v3 on v2

--- a/solution.py
+++ b/solution.py
@@ -11,11 +11,15 @@
 NCTX, NX, NZ, NHG = 32, 4, 8, 16
 TOK, HD, DIM, ROPE, LAT, SLOTS, COLS = 128, 8, 128, 64, 512, 768, 224
 PAIRS = HD // 2
-FACTOR = 1.0 / math.sqrt(DIM + ROPE)
+LOG2E = math.log2(math.e)
+FACTOR2 = LOG2E / math.sqrt(DIM + ROPE)
 MESH = pl.DeviceIdType.MESH
 F32, BF16 = jnp.float32, jnp.bfloat16
 NEAR_FIRST = (1, 7, 2, 6, 3, 5, 4)
 FAR_FIRST = (4, 3, 5, 2, 6, 1, 7)
+HOT = 2
+OWNER_ORDER = ((4, 2, 6, 0), (3, 5, 1, 7))
+PASS_ORDER = (0, 2, 4, 6, 1, 3, 5, 7)
 
 
 def rows(start, size):
@@ -28,7 +32,7 @@
     keys, values_t, kr, qa_all, qb_all, q_wide, r_wide, counts,
     o_mine, lse_mine, o_all, lse_all, a_all, part, part_all,
     load_sem, q_send, qz_recv, qx_recv, n_send, nz_recv, nx_recv,
-    o_send, o_recv, lse_send, lse_recv, a_send, az_recv, ax_recv, ab_recv, p_send, p_recv,
+    o_send, o_recv, lse_send, lse_recv, a_send, az_recv, ax_recv, p_send, p_recv,
 ):
     c, g = lax.axis_index("ctx"), lax.axis_index("hg")
     z, x = lax.rem(c, NZ), lax.div(c, NZ)
@@ -39,6 +43,9 @@
 
     def x_peer(k):
         return lax.rem(c + NZ * k, NCTX)
+
+    def zx_peer(k, j):
+        return lax.rem(z_peer(k) + NZ * j, NCTX)
 
     def h_peer(k):
         return lax.rem(g + k, NHG)
@@ -53,7 +60,7 @@
         pltpu.make_async_copy(ref, ref, sem).wait()
 
     barrier = pltpu.get_barrier_semaphore()
-    for k in range(1, NZ):
+    for k in FAR_FIRST:
         pl.semaphore_signal(barrier, inc=1, device_id=(z_peer(k), g), device_id_type=MESH)
     for k in range(1, NX):
         pl.semaphore_signal(barrier, inc=1, device_id=(x_peer(k), g), device_id_type=MESH)
@@ -89,14 +96,19 @@
     pl.semaphore_wait(barrier, (NZ - 1) + (NX - 1) + (NHG - 1))
 
     q_parts = ((qa_all, 32), (qb_all, 16))
+
+    def to_x(block, send_sem, x_sem):
+        for j in (2, 1, 3):
+            send(block, block, send_sem, x_sem, x_peer(j), g)
+
     for i, (ref, size) in enumerate(q_parts):
         block = ref.at[rows(c * size, size)]
         for k in FAR_FIRST:
             send(block, block, q_send.at[i], qz_recv.at[i, k], z_peer(k), g)
-            if i == 0:
+        to_x(block, q_send.at[i], qx_recv.at[i])
+        if i == 0:
+            for k in FAR_FIRST:
                 send(counts.at[c], counts.at[c], n_send, nz_recv, z_peer(k), g)
-        for j in (2, 1, 3):
-            send(block, block, q_send.at[i], qx_recv.at[i], x_peer(j), g)
 
     loads[4].wait()
     wide[...] = upk_v[...].astype(F32).reshape(LAT * HD, DIM)
@@ -129,13 +141,10 @@
         for k in NEAR_FIRST:
             block = ref.at[rows(z_peer(k) * size, size)]
             drain(block, qz_recv.at[i, NZ - k])
-            for j in (2, 1, 3):
-                send(block, block, q_send.at[i], qx_recv.at[i], x_peer(j), g)
+            to_x(block, q_send.at[i], qx_recv.at[i])
         if i == 0:
             drain(counts.at[pl.ds(0, NZ - 1)], nz_recv)
-            some = counts.at[rows(column, NZ)]
-            for j in (2, 1, 3):
-                send(some, some, n_send, nx_recv, x_peer(j), g)
+            to_x(counts.at[rows(column, NZ)], n_send, nx_recv)
 
     drain(counts.at[pl.ds(0, 24)], nx_recv)
     shard = lax.broadcasted_iota(jnp.int32, (NCTX, DIM), 0)
@@ -145,90 +154,122 @@
     limit = jnp.minimum(token + (span[0] + 1) - offset, count)
     slot = lax.broadcasted_iota(jnp.int32, (SLOTS, TOK), 0)
 
+    def scores_of(i, t):
+        p = lax.rem(x + 1 + t, NX)
+        mine = pl.ds(p, TOK, stride=PAIRS)
+        q = jnp.concatenate([q_wide[mine, :].astype(BF16), r_wide[mine, :].astype(BF16)], axis=1)
+        k_cat = jnp.concatenate([keys[2 * p + i], kr[i]], axis=1)
+        return lax.dot_general(k_cat, q, (((1,), (1,)), ((), ())), preferred_element_type=F32)
+
+    def weights_of(i, t, scores):
+        scores = jnp.where(slot < limit, scores, NEG)
+        top = jnp.max(scores, axis=0, keepdims=True)
+        weights = jnp.exp2((scores - top) * FACTOR2)
+        total = jnp.sum(weights, axis=0, keepdims=True)
+        lse_mine[i, lax.rem(x + 1 + t, NX)] = top * FACTOR2 + jnp.log(total) * LOG2E
+        return weights.astype(BF16), 1.0 / total
+
+    def values_of(i, t, weights, scale):
+        p = lax.rem(x + 1 + t, NX)
+        summed = jnp.dot(
+            values_t[rows((2 * p + i) * DIM, DIM), :], weights, preferred_element_type=F32
+        )
+        o_mine[i, rows(p * DIM, DIM), :] = (summed * scale).astype(BF16)
+
+    def give_out(i, t):
+        p = lax.rem(x + 1 + t, NX)
+        for zz in OWNER_ORDER[i]:
+            dst = p * NZ + zz
+            place = lax.rem(c - dst + NCTX, NCTX)
+            mine = rows((p * 4 + zz // 2) * 32, 32)
+
+            def go():
+                send(lse_mine.at[i, p], lse_all.at[place], lse_send, lse_recv, dst, g)
+                send(
+                    o_mine.at[i, mine], o_all.at[rows(place * 32, 32)], o_send, o_recv, dst, g
+                )
+
+            if t < PAIRS - 1:
+                go()
+            else:
+                pl.when(zz != z)(go)
+
     for i, (ref, size) in enumerate(q_parts):
         drain(ref.at[pl.ds(0, 24 * size)], qx_recv.at[i])
         got = ref[...].astype(F32).reshape(NCTX, size, DIM)
         q_wide[...] = got[:, 0:16].reshape(NCTX * 16, DIM)
         if i == 0:
             r_wide[...] = got[:, 16:32].reshape(NCTX * 16, DIM)
+        coming = scores_of(i, 0)
         for t in range(PAIRS):
-            p = lax.rem(x + 1 + t, NX)
-            h = 2 * p + i
-            mine = pl.ds(p, TOK, stride=PAIRS)
-            q = jnp.concatenate(
-                [q_wide[mine, :].astype(BF16), r_wide[mine, :].astype(BF16)], axis=1
-            )
-            k_cat = jnp.concatenate([keys[h], kr[i]], axis=1)
-            scores = lax.dot_general(
-                k_cat, q, (((1,), (1,)), ((), ())), preferred_element_type=F32
-            )
-            scores = jnp.where(slot < limit, scores, NEG)
-            top = jnp.max(scores, axis=0, keepdims=True)
-            weights = jnp.exp((scores - top) * FACTOR)
-            total = jnp.sum(weights, axis=0, keepdims=True)
-            lse_mine[i, p] = top * FACTOR + jnp.log(total)
-            summed = jnp.dot(
-                values_t[rows(h * DIM, DIM), :], weights.astype(BF16), preferred_element_type=F32
-            )
-            o_mine[i, rows(p * DIM, DIM), :] = (summed / total).astype(BF16)
-            for j in (4, 3, 5, 2, 6, 1, 7, 0):
-                if t == PAIRS - 1 and j == 0:
-                    continue
-                dst = p * NZ + lax.rem(z + j, NZ)
-                place = lax.rem(c - dst + NCTX, NCTX)
-                send(
-                    lse_mine.at[i, p], lse_all.at[i, place], lse_send.at[i], lse_recv.at[i], dst, g
-                )
-                send(
-                    o_mine.at[i, rows(dst * 16, 16)], o_all.at[i, rows(place * 16, 16)],
-                    o_send.at[i], o_recv.at[i], dst, g,
-                )
-
-    for i in range(2):
-        o_all[i, 0:16, :] = o_mine[i, mine16, :]
-        lse_all[i, 0] = lse_mine[i, x]
-        drain(lse_all.at[i, pl.ds(1, NCTX - 1)], lse_recv.at[i])
-        lse = lse_all[i, :, 0, :]
-        share = jnp.exp(lse - jnp.max(lse, axis=0, keepdims=True))
-        share = share / jnp.sum(share, axis=0, keepdims=True)
-        drain(o_all.at[i, pl.ds(16, (NCTX - 1) * 16)], o_recv.at[i])
-        joined = jnp.zeros((16, TOK), F32)
-        for s in range(NCTX):
-            joined = joined + o_all[i, s * 16 : (s + 1) * 16, :].astype(F32) * share[s : s + 1, :]
-        a_all[i, mine16, :] = joined.astype(BF16)
-        block = a_all.at[i, mine16]
-        if i == 0:
-            for k in FAR_FIRST:
-                send(block, block, a_send.at[i], az_recv.at[k], z_peer(k), g)
-            for j in (2, 1, 3):
-                send(block, block, a_send.at[i], ax_recv, x_peer(j), g)
-        else:
-            for k in FAR_FIRST + (0,):
-                for j in (2, 1, 3, 0):
-                    if k or j:
-                        dst = lax.rem(z_peer(k) + NZ * j, NCTX)
-                        send(block, block, a_send.at[i], ab_recv, dst, g)
-    for k in NEAR_FIRST:
-        block = a_all.at[0, rows(z_peer(k) * 16, 16)]
-        drain(block, az_recv.at[NZ - k])
+            scores = coming
+            if t < PAIRS - 1:
+                coming = scores_of(i, t + 1)
+            values_of(i, t, *weights_of(i, t, scores))
+            give_out(i, t)
+
+    group, place = lax.rem(z, 2), x * 4 + lax.div(z, 2)
+    own = rows(place * 32, 32)
+    o_all[0:32, :] = o_mine[group, own, :]
+    lse_all[0] = lse_mine[group, x]
+    drain(lse_all.at[pl.ds(1, NCTX - 1)], lse_recv)
+    lse = lse_all[:, 0, :]
+    share = jnp.exp2(lse - jnp.max(lse, axis=0, keepdims=True))
+    share = share / jnp.sum(share, axis=0, keepdims=True)
+    drain(o_all.at[pl.ds(32, (NCTX - 1) * 32)], o_recv)
+    joined = jnp.zeros((32, TOK), F32)
+    for s in range(NCTX):
+        joined = joined + o_all[s * 32 : (s + 1) * 32, :].astype(F32) * share[s : s + 1, :]
+    a_all[group, own, :] = joined.astype(BF16)
+    block = a_all.at[group, own]
+    for zz in range(HOT):
+        @pl.when(z != zz)
+        def _():
+            send(block, block, a_send, az_recv.at[z], column + zz, g)
+
         for j in (2, 1, 3):
-            send(block, block, a_send.at[0], ax_recv, x_peer(j), g)
+            dst = lax.rem(column + NZ * j, NCTX) + zz
+            send(block, block, a_send, ax_recv.at[group], dst, g)
+    for k in FAR_FIRST:
+        @pl.when(lax.rem(z + k, NZ) >= HOT)
+        def _():
+            send(block, block, a_send, az_recv.at[z], z_peer(k), g)
+
+    @pl.when(z >= HOT)
+    def _():
+        to_x(block, a_send, ax_recv.at[group])
+
+    def pass_on(zz):
+        @pl.when(zz != z)
+        def _():
+            block = a_all.at[zz % 2, rows((x * 4 + zz // 2) * 32, 32)]
+            drain(block, az_recv.at[zz])
+
+            @pl.when(z >= HOT)
+            def _():
+                to_x(block, a_send, ax_recv.at[zz % 2])
 
     loads[8].wait()
     w = [jnp.concatenate([wt_v[2 * p + i] for p in range(PAIRS)], axis=1) for i in range(2)]
-    drain(a_all.at[0, pl.ds(0, 24 * 16)], ax_recv)
+    for zz in PASS_ORDER:
+        pass_on(zz)
+    drain(a_all.at[0, pl.ds(0, 12 * 32)], ax_recv.at[0])
     mixed_t = jnp.dot(w[0], a_all[0], preferred_element_type=F32)
-    drain(a_all.at[1, pl.ds(0, (NCTX - 1) * 16)], ab_recv)
+    drain(a_all.at[1, pl.ds(0, 12 * 32)], ax_recv.at[1])
     mixed_t = mixed_t + jnp.dot(w[1], a_all[1], preferred_element_type=F32)
     mixed_t = jnp.concatenate([mixed_t, jnp.zeros((256 - COLS, TOK), F32)], axis=0)
     left = mixed_t[0:128].T.reshape(NHG, 8, 128)
     right = mixed_t[128:].T.reshape(NHG, 8, 128)
     part[...] = jnp.concatenate([left, right], axis=1).astype(BF16).reshape(NHG * 16, 128)
-    for k in (8, 9, 7, 10, 6, 11, 5, 12, 4, 13, 3, 14, 2, 15, 1):
-        send(
-            part.at[rows(h_peer(k) * 16, 16)], part_all.at[pl.ds((NHG - k) * 16, 16)],
-            p_send, p_recv, c, h_peer(k),
-        )
+    for dst in (0, 1, 8, 9, 6, 7, 10, 11, 4, 5, 12, 13, 2, 3, 14, 15):
+        @pl.when(g != dst)
+        def _():
+            place = lax.rem(g - dst + NHG, NHG)
+            send(
+                part.at[dst * 16 : (dst + 1) * 16], part_all.at[rows(place * 16, 16)],
+                p_send, p_recv, c, dst,
+            )
+
     acc = part[rows(g * 16, 16), :].astype(F32)
     drain(part_all.at[pl.ds(16, (NHG - 1) * 16)], p_recv)
     for k in range(1, NHG):
@@ -237,9 +278,14 @@
 
     for i, (ref, size) in enumerate(q_parts):
         drain(ref.at[pl.ds(0, 31 * size)], q_send.at[i])
-        drain(o_all.at[i, pl.ds(16, (NCTX - 1) * 16)], o_send.at[i])
-        drain(lse_all.at[i, pl.ds(1, NCTX - 1)], lse_send.at[i])
-        drain(a_all.at[i, pl.ds(0, (NCTX - 1) * 16)], a_send.at[i])
+    drain(o_all.at[pl.ds(32, (NCTX - 1) * 32)], o_send)
+    drain(lse_all.at[pl.ds(1, NCTX - 1)], lse_send)
+    drain(o_all.at[pl.ds(0, (NZ - 1 + 3 * HOT) * 32)], a_send)
+
+    @pl.when(z >= HOT)
+    def _():
+        drain(o_all.at[pl.ds(0, 24 * 32)], a_send)
+
     drain(counts.at[pl.ds(0, 31)], n_send)
     drain(part_all.at[pl.ds(16, (NHG - 1) * 16)], p_send)
 
@@ -278,13 +324,13 @@
             pltpu.VMEM((NCTX, 1, DIM), F32),
             pltpu.VMEM((2, PAIRS * DIM, TOK), BF16),
             pltpu.VMEM((2, PAIRS, 1, TOK), F32),
-            pltpu.VMEM((2, NCTX * 16, TOK), BF16),
-            pltpu.VMEM((2, NCTX, 1, TOK), F32),
+            pltpu.VMEM((NCTX * 32, TOK), BF16),
+            pltpu.VMEM((NCTX, 1, TOK), F32),
             pltpu.VMEM((2, PAIRS * DIM, TOK), BF16),
             pltpu.VMEM((NHG * 16, 128), BF16),
             pltpu.VMEM((NHG * 16, 128), BF16),
             dma((9,)), dma((2,)), dma((2, NZ)), dma((2,)), dma, dma, dma,
-            dma((2,)), dma((2,)), dma((2,)), dma((2,)), dma((2,)), dma((NZ,)), dma, dma, dma, dma,
+            dma, dma, dma, dma, dma, dma((NZ,)), dma((2,)), dma, dma,
         ],
         compiler_params=pltpu.CompilerParams(
             collective_id=0, has_side_effects=True, vmem_limit_bytes=48 * 1024 * 1024

time: 48.7 us -> 47.2 us (0.969)
  Pallas kernels: 46.7 us -> 45.1 us
    pallas_call x1, Pallas kernels: 46.7 us -> 45.1 us  [per_device(): call(live_rows, span_start, *[pltpu.with_memory_space_constraint(a, pltpu...]
where the time goes in v3:
time: 47.2 us; the launch traced here: 47 us
  Pallas kernels  45.1 us (96%)
  between operations  1.3 us (3%)
  local copies, waits for them, and re-layouts  0.6 us (1%)
    pallas_call x1, Pallas kernels, per_device(): call(live_rows, span_start, *[pltpu.with_memory_space_constraint(a, pltpu...  45.1 us

profile of v3, /device:TPU:1, one launch (start us, length us, event | category | flops | bytes accessed | tf_op | source)
XLA Modules:
  0.0 47.0 jit_solution(14441499372542391089)
XLA Ops:
  1.3 45.1 %shard_map.91 = bf16[8,224]{1,0:T(8,128)(2,1)S(1)} custom-call(s32[1]{0:T(128)S(6)} %copy.11.live_h, s32[1]{0:T(128)S(6)} %copy.12.span_h, bf16[4,8,128]{2,1,0:T(8,128)(2,1)} %qn_h.1, bf16[4,8,64]{2,1,0:T(8,128)(2,1)} %qr_h.1, bf16[768,512]{1,0:T(8,128)(2,1)} %latent.1, bf16[64,768]{1,0:T(8,128)(2,1)} %bitcast.3, bf16[512,8,128]{2,1,0:T(8,128)(2,1)} %up_k.1, ...), custom_call_target="tpu_custom_call" | custom-call | tf_op jit(solution)/shard_map/pallas_call | solution.py:343
  46.4 0.6 %copy.13 = bf16[8,224]{1,0:T(8,128)(2,1)} copy(bf16[8,224]{1,0:T(8,128)(2,1)S(1)} %shard_map.91) | data formatting | bytes 7168

commit v4 on v3

--- a/solution.py
+++ b/solution.py
@@ -18,6 +18,7 @@
 NEAR_FIRST = (1, 7, 2, 6, 3, 5, 4)
 FAR_FIRST = (4, 3, 5, 2, 6, 1, 7)
 HOT = 2
+VIA_X = (1, 7, 2, 6)
 OWNER_ORDER = ((4, 2, 6, 0), (3, 5, 1, 7))
 PASS_ORDER = (0, 2, 4, 6, 1, 3, 5, 7)
 
@@ -31,7 +32,7 @@
     live, span, qn, qr, lat_v, rope_v, upk_v, upv_v, wt_v, small, wide, wk, wvt,
     keys, values_t, kr, qa_all, qb_all, q_wide, r_wide, counts,
     o_mine, lse_mine, o_all, lse_all, a_all, part, part_all,
-    load_sem, q_send, qz_recv, qx_recv, n_send, nz_recv, nx_recv,
+    load_sem, q_send, qz_recv, qx_recv, q2_recv, n_send, nz_recv, nx_recv,
     o_send, o_recv, lse_send, lse_recv, a_send, az_recv, ax_recv, p_send, p_recv,
 ):
     c, g = lax.axis_index("ctx"), lax.axis_index("hg")
@@ -105,7 +106,9 @@
         block = ref.at[rows(c * size, size)]
         for k in FAR_FIRST:
             send(block, block, q_send.at[i], qz_recv.at[i, k], z_peer(k), g)
-        to_x(block, q_send.at[i], qx_recv.at[i])
+        send(block, block, q_send.at[i], q2_recv.at[i], x_peer(2), g)
+        for j in (1, 3):
+            send(block, block, q_send.at[i], qx_recv.at[i], x_peer(j), g)
         if i == 0:
             for k in FAR_FIRST:
                 send(counts.at[c], counts.at[c], n_send, nz_recv, z_peer(k), g)
@@ -141,7 +144,13 @@
         for k in NEAR_FIRST:
             block = ref.at[rows(z_peer(k) * size, size)]
             drain(block, qz_recv.at[i, NZ - k])
-            to_x(block, q_send.at[i], qx_recv.at[i])
+            for j in (1, 3) if NZ - k in VIA_X else (2, 1, 3):
+                send(block, block, q_send.at[i], qx_recv.at[i], x_peer(j), g)
+            if k == 6:
+                across = ref.at[rows(x_peer(2) * size, size)]
+                drain(across, q2_recv.at[i])
+                for near in VIA_X:
+                    send(across, across, q_send.at[i], qx_recv.at[i], z_peer(near), g)
         if i == 0:
             drain(counts.at[pl.ds(0, NZ - 1)], nz_recv)
             to_x(counts.at[rows(column, NZ)], n_send, nx_recv)
@@ -195,7 +204,7 @@
                 pl.when(zz != z)(go)
 
     for i, (ref, size) in enumerate(q_parts):
-        drain(ref.at[pl.ds(0, 24 * size)], qx_recv.at[i])
+        drain(ref.at[pl.ds(0, 23 * size)], qx_recv.at[i])
         got = ref[...].astype(F32).reshape(NCTX, size, DIM)
         q_wide[...] = got[:, 0:16].reshape(NCTX * 16, DIM)
         if i == 0:
@@ -329,7 +338,7 @@
             pltpu.VMEM((2, PAIRS * DIM, TOK), BF16),
             pltpu.VMEM((NHG * 16, 128), BF16),
             pltpu.VMEM((NHG * 16, 128), BF16),
-            dma((9,)), dma((2,)), dma((2, NZ)), dma((2,)), dma, dma, dma,
+            dma((9,)), dma((2,)), dma((2, NZ)), dma((2,)), dma((2,)), dma, dma, dma,
             dma, dma, dma, dma, dma, dma((NZ,)), dma((2,)), dma, dma,
         ],
         compiler_params=pltpu.CompilerParams(

time: 47.2 us -> 46.8 us (level)
  no operation moved by 1% of the time
where the time goes in v4:
time: 46.8 us; the launch traced here: 46.6 us
  Pallas kernels  44.7 us (96%)
  between operations  1.3 us (3%)
  local copies, waits for them, and re-layouts  0.6 us (1%)
    pallas_call x1, Pallas kernels, per_device(): call(live_rows, span_start, *[pltpu.with_memory_space_constraint(a, pltpu...  44.7 us

profile of v4, /device:TPU:1, one launch (start us, length us, event | category | flops | bytes accessed | tf_op | source)
XLA Modules:
  0.0 46.6 jit_solution(15057095740568951521)
XLA Ops:
  1.3 44.7 %shard_map.91 = bf16[8,224]{1,0:T(8,128)(2,1)S(1)} custom-call(s32[1]{0:T(128)S(6)} %copy.11.live_h, s32[1]{0:T(128)S(6)} %copy.12.span_h, bf16[4,8,128]{2,1,0:T(8,128)(2,1)} %qn_h.1, bf16[4,8,64]{2,1,0:T(8,128)(2,1)} %qr_h.1, bf16[768,512]{1,0:T(8,128)(2,1)} %latent.1, bf16[64,768]{1,0:T(8,128)(2,1)} %bitcast.3, bf16[512,8,128]{2,1,0:T(8,128)(2,1)} %up_k.1, ...), custom_call_target="tpu_custom_call" | custom-call | tf_op jit(solution)/shard_map/pallas_call | solution.py:352
  46.0 0.6 %copy.13 = bf16[8,224]{1,0:T(8,128)(2,1)} copy(bf16[8,224]{1,0:T(8,128)(2,1)S(1)} %shard_map.91) | data formatting | bytes 7168

commit v5 on v4

--- a/solution.py
+++ b/solution.py
@@ -20,7 +20,7 @@
 HOT = 2
 VIA_X = (1, 7, 2, 6)
 OWNER_ORDER = ((4, 2, 6, 0), (3, 5, 1, 7))
-PASS_ORDER = (0, 2, 4, 6, 1, 3, 5, 7)
+PASS_ORDER = (1, 7, 2, 6, 3, 5, 4)
 
 
 def rows(start, size):
@@ -248,20 +248,20 @@
     def _():
         to_x(block, a_send, ax_recv.at[group])
 
-    def pass_on(zz):
-        @pl.when(zz != z)
+    def pass_on(k):
+        zz = lax.rem(z + k, NZ)
+        group = lax.rem(zz, 2)
+        block = a_all.at[group, rows((x * 4 + lax.div(zz, 2)) * 32, 32)]
+        drain(block, az_recv.at[zz])
+
+        @pl.when(z >= HOT)
         def _():
-            block = a_all.at[zz % 2, rows((x * 4 + zz // 2) * 32, 32)]
-            drain(block, az_recv.at[zz])
-
-            @pl.when(z >= HOT)
-            def _():
-                to_x(block, a_send, ax_recv.at[zz % 2])
+            to_x(block, a_send, ax_recv.at[group])
 
     loads[8].wait()
     w = [jnp.concatenate([wt_v[2 * p + i] for p in range(PAIRS)], axis=1) for i in range(2)]
-    for zz in PASS_ORDER:
-        pass_on(zz)
+    for k in PASS_ORDER:
+        pass_on(k)
     drain(a_all.at[0, pl.ds(0, 12 * 32)], ax_recv.at[0])
     mixed_t = jnp.dot(w[0], a_all[0], preferred_element_type=F32)
     drain(a_all.at[1, pl.ds(0, 12 * 32)], ax_recv.at[1])

time: 46.8 us -> 46.8 us (level)
  no operation moved by 1% of the time
where the time goes in v5:
time: 46.8 us; the launch traced here: 46.6 us
  Pallas kernels  44.7 us (96%)
  between operations  1.3 us (3%)
  local copies, waits for them, and re-layouts  0.6 us (1%)
    pallas_call x1, Pallas kernels, per_device(): call(live_rows, span_start, *[pltpu.with_memory_space_constraint(a, pltpu...  44.7 us

profile of v5, /device:TPU:1, one launch (start us, length us, event | category | flops | bytes accessed | tf_op | source)
XLA Modules:
  0.0 46.6 jit_solution(17483789143417615420)
XLA Ops:
  1.3 44.7 %shard_map.91 = bf16[8,224]{1,0:T(8,128)(2,1)S(1)} custom-call(s32[1]{0:T(128)S(6)} %copy.11.live_h, s32[1]{0:T(128)S(6)} %copy.12.span_h, bf16[4,8,128]{2,1,0:T(8,128)(2,1)} %qn_h.1, bf16[4,8,64]{2,1,0:T(8,128)(2,1)} %qr_h.1, bf16[768,512]{1,0:T(8,128)(2,1)} %latent.1, bf16[64,768]{1,0:T(8,128)(2,1)} %bitcast.3, bf16[512,8,128]{2,1,0:T(8,128)(2,1)} %up_k.1, ...), custom_call_target="tpu_custom_call" | custom-call | tf_op jit(solution)/shard_map/pallas_call | solution.py:352
  46.0 0.6 %copy.13 = bf16[8,224]{1,0:T(8,128)(2,1)} copy(bf16[8,224]{1,0:T(8,128)(2,1)S(1)} %shard_map.91) | data formatting | bytes 7168

commit v6 on v5

--- a/solution.py
+++ b/solution.py
@@ -17,7 +17,7 @@
 F32, BF16 = jnp.float32, jnp.bfloat16
 NEAR_FIRST = (1, 7, 2, 6, 3, 5, 4)
 FAR_FIRST = (4, 3, 5, 2, 6, 1, 7)
-HOT = 2
+HOT = 3
 VIA_X = (1, 7, 2, 6)
 OWNER_ORDER = ((4, 2, 6, 0), (3, 5, 1, 7))
 PASS_ORDER = (1, 7, 2, 6, 3, 5, 4)

time: 46.8 us -> 46.8 us (level)
  no operation moved by 1% of the time
where the time goes in v6:
time: 46.8 us; the launch traced here: 46.6 us
  Pallas kernels  44.7 us (96%)
  between operations  1.3 us (3%)
  local copies, waits for them, and re-layouts  0.6 us (1%)
    pallas_call x1, Pallas kernels, per_device(): call(live_rows, span_start, *[pltpu.with_memory_space_constraint(a, pltpu...  44.7 us

profile of v6, /device:TPU:1, one launch (start us, length us, event | category | flops | bytes accessed | tf_op | source)
XLA Modules:
  0.0 46.6 jit_solution(11636781800443181634)
XLA Ops:
  1.3 44.7 %shard_map.91 = bf16[8,224]{1,0:T(8,128)(2,1)S(1)} custom-call(s32[1]{0:T(128)S(6)} %copy.11.live_h, s32[1]{0:T(128)S(6)} %copy.12.span_h, bf16[4,8,128]{2,1,0:T(8,128)(2,1)} %qn_h.1, bf16[4,8,64]{2,1,0:T(8,128)(2,1)} %qr_h.1, bf16[768,512]{1,0:T(8,128)(2,1)} %latent.1, bf16[64,768]{1,0:T(8,128)(2,1)} %bitcast.3, bf16[512,8,128]{2,1,0:T(8,128)(2,1)} %up_k.1, ...), custom_call_target="tpu_custom_call" | custom-call | tf_op jit(solution)/shard_map/pallas_call | solution.py:352
  46.0 0.6 %copy.13 = bf16[8,224]{1,0:T(8,128)(2,1)} copy(bf16[8,224]{1,0:T(8,128)(2,1)S(1)} %shard_map.91) | data formatting | bytes 7168
